TPU v7x, 256 devices: a whole 4x4x8 slice. The times are simulated.
256 devices in a mesh: dp: 8 (over x, y_hi), expert: 32 (over z, y_lo, core).
Axes of the slice: x: 4, y: 4 (y_hi: 2, y_lo: 2; y = y_hi * 2 + y_lo), z: 8, core: 2. Of those that a mesh axis runs over, the one named last changes fastest.
Arguments:
- tokens: bfloat16 [3072, 4096], P(('dp', 'expert')), may hold values from -6 to 6
- expert_ids: int32 [3072, 8], P(('dp', 'expert')), may hold values from 0 to 63, all different within a row; in each aligned block of 12 rows (0 to 11, 12 to 23, ...) at most 3 rows name the same one
- gate_probs: float32 [3072, 8], P(('dp', 'expert')), may hold values from 0.02 to 5
- in_weight: bfloat16 [64, 4096, 3072], P('expert', None, 'dp'), may hold values from -0.09375 to 0.09375
- out_weight: bfloat16 [64, 1536, 4096], P('expert', 'dp'), may hold values from -0.15625 to 0.15625
- swap_slot: int32 [32], replicated, may hold values from 0 to 1
Outputs:
- mixed_out: bfloat16 [3072, 4096], P(('dp', 'expert'))
- owner_load: float32 [32], replicated
Inputs may be any that keep to these rules, and one draw needn't show every extreme that they name: `expert_ids`: among the rows of one device no expert is named more than 3 times, and in every draw some device's rows name some expert exactly 3 times; a row names 8 different experts.
All inputs are finite; a program needn't handle non-finite values.
Results may differ from a plain program's by a relative error of at most 0.018.
Values may be sent and summed in bfloat16 or wider, within the bound.
A program may use at most 128 MiB of HBM per device.

v0:
```python
import jax
import jax.numpy as jnp
from jax import lax
from jax.sharding import PartitionSpec as P

BOTH = ("dp", "expert")


def planned_load(mass, swap_slot, per_device, owners, tokens_all):
    experts = jnp.arange(mass.shape[0], dtype=jnp.int32)
    home, within = (experts // per_device, experts % per_device)
    slot = jnp.repeat(swap_slot, per_device)
    holder = jnp.where(within == slot, (home + owners // 2) % owners, home)
    hot = holder[:, None] == jnp.arange(owners, dtype=jnp.int32)
    return jnp.sum(jnp.where(hot, mass[:, None], 0.0), 0) * (owners / tokens_all)


def on_device(tokens, expert_ids, gate_probs, in_weight, out_weight, swap_slot):
    owners = lax.axis_size("expert")
    per_device, width = in_weight.shape[:2]
    half = out_weight.shape[1]
    experts_all = per_device * owners
    experts = jnp.arange(experts_all, dtype=jnp.int32)
    dense = jnp.sum(jnp.where(expert_ids[..., None] == experts, gate_probs[..., None], 0.0), 1)
    all_tokens = lax.all_gather(tokens, BOTH, axis=0, tiled=True)
    all_dense = lax.all_gather(dense, BOTH, axis=0, tiled=True)
    load = planned_load(jnp.sum(all_dense, 0), swap_slot, per_device, owners, all_tokens.shape[0])
    mine = lax.dynamic_slice_in_dim(all_dense, lax.axis_index("expert") * per_device, per_device, 1)
    parts = []
    for s in range(per_device):
        both = jnp.dot(all_tokens, in_weight[s], preferred_element_type=jnp.float32)
        hidden = jax.nn.silu(both[:, :half]) * both[:, half:] * mine[:, s : s + 1]
        parts.append(hidden.astype(jnp.bfloat16))
    mixed = jnp.dot(
        jnp.concatenate(parts, 1),
        out_weight.reshape(per_device * half, width),
        preferred_element_type=jnp.float32,
    ).astype(jnp.bfloat16)
    out = lax.psum_scatter(mixed, BOTH, scatter_dimension=0, tiled=True)
    return (out, load)


def solution(mesh):
    return jax.shard_map(
        on_device,
        mesh=mesh,
        in_specs=(
            P(BOTH, None),
            P(BOTH, None),
            P(BOTH, None),
            P("expert", None, "dp"),
            P("expert", "dp", None),
            P(),
        ),
        out_specs=(P(BOTH, None), P()),
        check_vma=False,
    )
```

profile of v0, /device:TPU:6, one launch (start us, length us, event | category | flops | bytes accessed | tf_op | source)
XLA Modules:
  0.0 2044.4 jit_solution(17175509425682315164)
XLA Ops:
  9.8 336.8 %all-gather.1 = f32[256,12,64]{2,1,0:T(8,128)} all-gather(f32[1,12,64]{2,1,0:T(8,128)S(1)} %bitcast.14), channel_id=1, replica_groups=mesh['dp'=8,'expert'=32] {'dp','expert'}, dimensions={0}, use_global_device_ids=true | all-gather | bytes 789504 | tf_op jit(solution)/shard_map/all_gather | solution.py:26
  346.6 2.5 reshape.56
  349.1 3.6 dynamic-slice_reduce_fusion.1
  352.7 104.2 %all-gather.4.cloned.1.call-done = bf16[256,12,4096]{2,1,0:T(8,128)(2,1)} async-done(((bf16[1,12,4096]{2,1,0:T(8,128)(2,1)}), bf16[256,12,4096]{2,1,0:T(8,128)(2,1)}) %all-gather.4.cloned.1.call-update) | async-done | bytes 25165840 | tf_op jit(solution)/shard_map/all_gather | solution.py:25
  457.0 34.8 %reshape.54 = bf16[3072,4096]{1,0:T(8,128)(2,1)} reshape(bf16[256,12,4096]{2,1,0:T(8,128)(2,1)} %all-gather.4.cloned.1.call-done) | data formatting | bytes 50331648
  491.8 14.5 fusion.1
  506.3 16.3 fusion.3
  522.6 4.3 fusion.8
  526.8 18.4 convolution_convert_fusion
  545.3 661.3 %fusion = bf16[16,4096]{1,0:T(8,128)(2,1)S(1)} fusion(bf16[3072,4096]{1,0:T(8,128)(2,1)} %convolution_convert_fusion), kind=kCustom, calls=%all-reduce-scatter | all-reduce-scatter fusion | flops 16777216 | bytes 25296896
  1206.6 77.1 %collective-permute-start.62 = (bf16[16,4096]{1,0:T(8,128)(2,1)S(1)}, bf16[16,4096]{1,0:T(8,128)(2,1)S(1)}, u32[]{:S(2)}, u32[]{:S(2)}) collective-permute-start(bf16[16,4096]{1,0:T(8,128)(2,1)S(1)} %fusion), channel_id=1, source_target_pairs={{0,63},{1,64},{2,65},{3,66},{4,67},{5,68},{6,69},{7,70},{8,71},{9,... | collective-permute-start | bytes 393224
  1283.7 1.9 collective-permute-start.61
  1285.6 1.9 collective-permute-start.60
  1288.9 1.9 collective-permute-start.59
  1290.8 7.3 collective-permute-done.63
  1300.0 1.9 collective-permute-start.57
  1302.0 1.9 collective-permute-start.56
  1305.9 1.9 collective-permute-start.54
  1311.1 25.9 %collective-permute-done.57 = bf16[16,4096]{1,0:T(8,128)(2,1)S(1)} collective-permute-done((bf16[16,4096]{1,0:T(8,128)(2,1)S(1)}, bf16[16,4096]{1,0:T(8,128)(2,1)S(1)}, u32[]{:S(2)}, u32[]{:S(2)}) %collective-permute-start.57) | collective-permute-done | bytes 131104
  1338.9 16.6 collective-permute-done.56
  1365.9 4.6 collective-permute-done.52
  1372.4 2.3 collective-permute-done.51
  1378.6 1.9 collective-permute-start.44
  1385.6 5.4 collective-permute-done.46
  1392.9 16.0 collective-permute-done.45
  1410.8 3.9 collective-permute-done.44
  1416.6 1.9 collective-permute-start.38
  1418.5 8.6 collective-permute-done.42
  1432.0 7.6 collective-permute-done.40
  1446.1 7.1 collective-permute-done.37
  1460.5 1.9 collective-permute-start.29
  1462.4 5.6 collective-permute-done.33
  1468.1 22.1 %collective-permute-start.28 = (bf16[16,4096]{1,0:T(8,128)(2,1)S(1)}, bf16[16,4096]{1,0:T(8,128)(2,1)S(1)}, u32[]{:S(2)}, u32[]{:S(2)}) collective-permute-start(bf16[16,4096]{1,0:T(8,128)(2,1)S(1)} %fusion), channel_id=1, source_target_pairs={{0,29},{1,30},{2,31},{3,32},{4,33},{5,34},{6,35},{7,36},{8,37},{9,... | collective-permute-start | bytes 393224
  1490.2 13.1 collective-permute-start.27
  1503.4 13.1 collective-permute-start.26
  1516.5 13.1 collective-permute-start.25
  1529.7 13.1 collective-permute-start.24
  1542.8 13.1 collective-permute-start.23
  1556.0 13.1 collective-permute-start.22
  1569.1 13.1 collective-permute-start.21
  1582.3 13.1 collective-permute-start.20
  1595.4 13.1 collective-permute-start.19
  1608.6 13.1 collective-permute-start.18
  1621.7 13.1 collective-permute-start.17
  1634.9 13.1 collective-permute-start.16
  1648.0 13.1 collective-permute-start.15
  1661.2 13.1 collective-permute-start.14
  1674.3 13.1 collective-permute-start.13
  1687.4 13.1 collective-permute-start.12
  1700.6 13.1 collective-permute-start.11
  1714.1 13.1 collective-permute-start.10
  1728.6 13.1 collective-permute-start.9
  1741.7 13.1 collective-permute-start.8
  1754.9 13.1 collective-permute-start.7
  1768.0 13.1 collective-permute-start.6
  1781.1 13.1 collective-permute-start.5
  1794.9 2.1 reduce_sum.28
  1797.2 13.1 collective-permute-start.4
  1810.3 13.1 collective-permute-start.3
  1823.5 13.1 collective-permute-start.2
  1836.6 13.1 collective-permute-start.1
  1849.8 13.1 collective-permute-start
  1864.8 7.6 collective-permute-done
  1872.4 163.5 %concatenate.4 = bf16[1036,4096]{1,0:T(8,128)(2,1)} concatenate(bf16[12,4096]{1,0:T(8,128)(2,1)} %copy-done.2, bf16[16,4096]{1,0:T(8,128)(2,1)S(1)} %collective-permute-done.62, bf16[16,4096]{1,0:T(8,128)(2,1)S(1)} %collective-permute-done.61, bf16[16,4096]{1,0:T(8,128)(2,1)} %copy-done.1, bf16[16,4096]{1,0:T(8,128)(2,1)} %copy-done.3, bf16[16,4096]{1,0:T(8,128)(2,1)} %copy-done.4, ...), dimensions={0} | concatenate | bytes 16973824
  (176 shorter events, 64.1 us)
Async XLA Ops:
  7.2 449.8 %all-gather.4.cloned.1.call-start = ((), (), s32[]{:S(2)}) async-start(), calls=%async_computation | async-start | bytes 33685504 | tf_op jit(solution)/shard_map/all_gather | solution.py:25
  1206.6 93.4 %collective-permute-start.62 = (bf16[16,4096]{1,0:T(8,128)(2,1)S(1)}, bf16[16,4096]{1,0:T(8,128)(2,1)S(1)}, u32[]{:S(2)}, u32[]{:S(2)}) collective-permute-start(bf16[16,4096]{1,0:T(8,128)(2,1)S(1)} %fusion), channel_id=1, source_target_pairs={{0,63},{1,64},{2,65},{3,66},{4,67},{5,68},{6,69},{7,70},{8,71},{9,... | collective-permute-start | bytes 393224
  1283.7 18.3 collective-permute-start.61
  1285.6 18.3 collective-permute-start.60
  1288.9 16.9 collective-permute-start.59
  1298.1 11.1 collective-permute-start.58
  1300.0 37.0 %collective-permute-start.57 = (bf16[16,4096]{1,0:T(8,128)(2,1)S(1)}, bf16[16,4096]{1,0:T(8,128)(2,1)S(1)}, u32[]{:S(2)}, u32[]{:S(2)}) collective-permute-start(bf16[16,4096]{1,0:T(8,128)(2,1)S(1)} %fusion), channel_id=1, source_target_pairs={{0,58},{1,59},{2,60},{3,61},{4,62},{5,63},{6,64},{7,65},{8,66},{9,... | collective-permute-start | bytes 393224
  1302.0 53.6 %collective-permute-start.56 = (bf16[16,4096]{1,0:T(8,128)(2,1)S(1)}, bf16[16,4096]{1,0:T(8,128)(2,1)S(1)}, u32[]{:S(2)}, u32[]{:S(2)}) collective-permute-start(bf16[16,4096]{1,0:T(8,128)(2,1)S(1)} %fusion), channel_id=1, source_target_pairs={{0,57},{1,58},{2,59},{3,60},{4,61},{5,62},{6,63},{7,64},{8,65},{9,... | collective-permute-start | bytes 393224
  1303.9 54.5 %collective-permute-start.55 = (bf16[16,4096]{1,0:T(8,128)(2,1)S(1)}, bf16[16,4096]{1,0:T(8,128)(2,1)S(1)}, u32[]{:S(2)}, u32[]{:S(2)}) collective-permute-start(bf16[16,4096]{1,0:T(8,128)(2,1)S(1)} %fusion), channel_id=1, source_target_pairs={{0,56},{1,57},{2,58},{3,59},{4,60},{5,61},{6,62},{7,63},{8,64},{9,... | collective-permute-start | bytes 393224
  1305.9 55.3 %collective-permute-start.54 = (bf16[16,4096]{1,0:T(8,128)(2,1)S(1)}, bf16[16,4096]{1,0:T(8,128)(2,1)S(1)}, u32[]{:S(2)}, u32[]{:S(2)}) collective-permute-start(bf16[16,4096]{1,0:T(8,128)(2,1)S(1)} %fusion), channel_id=1, source_target_pairs={{0,55},{1,56},{2,57},{3,58},{4,59},{5,60},{6,61},{7,62},{8,63},{9,... | collective-permute-start | bytes 393224
  1309.2 54.8 %collective-permute-start.53 = (bf16[16,4096]{1,0:T(8,128)(2,1)S(1)}, bf16[16,4096]{1,0:T(8,128)(2,1)S(1)}, u32[]{:S(2)}, u32[]{:S(2)}) collective-permute-start(bf16[16,4096]{1,0:T(8,128)(2,1)S(1)} %fusion), channel_id=1, source_target_pairs={{0,54},{1,55},{2,56},{3,57},{4,58},{5,59},{6,60},{7,61},{8,62},{9,... | collective-permute-start | bytes 393224
  1337.0 33.5 %collective-permute-start.52 = (bf16[16,4096]{1,0:T(8,128)(2,1)S(1)}, bf16[16,4096]{1,0:T(8,128)(2,1)S(1)}, u32[]{:S(2)}, u32[]{:S(2)}) collective-permute-start(bf16[16,4096]{1,0:T(8,128)(2,1)S(1)} %fusion), channel_id=1, source_target_pairs={{0,53},{1,54},{2,55},{3,56},{4,57},{5,58},{6,59},{7,60},{8,61},{9,... | collective-permute-start | bytes 393224
  1355.6 19.1 collective-permute-start.51
  1358.4 18.2 collective-permute-start.50
  1361.2 17.4 collective-permute-start.49
  1364.0 16.5 collective-permute-start.48
  1370.5 13.2 collective-permute-start.47
  1374.7 16.3 collective-permute-start.46
  1376.6 32.3 %collective-permute-start.45 = (bf16[16,4096]{1,0:T(8,128)(2,1)S(1)}, bf16[16,4096]{1,0:T(8,128)(2,1)S(1)}, u32[]{:S(2)}, u32[]{:S(2)}) collective-permute-start(bf16[16,4096]{1,0:T(8,128)(2,1)S(1)} %fusion), channel_id=1, source_target_pairs={{0,46},{1,47},{2,48},{3,49},{4,50},{5,51},{6,52},{7,53},{8,54},{9,... | collective-permute-start | bytes 393224
  1378.6 36.1 %collective-permute-start.44 = (bf16[16,4096]{1,0:T(8,128)(2,1)S(1)}, bf16[16,4096]{1,0:T(8,128)(2,1)S(1)}, u32[]{:S(2)}, u32[]{:S(2)}) collective-permute-start(bf16[16,4096]{1,0:T(8,128)(2,1)S(1)} %fusion), channel_id=1, source_target_pairs={{0,45},{1,46},{2,47},{3,48},{4,49},{5,50},{6,51},{7,52},{8,53},{9,... | collective-permute-start | bytes 393224
  1380.5 36.1 %collective-permute-start.43 = (bf16[16,4096]{1,0:T(8,128)(2,1)S(1)}, bf16[16,4096]{1,0:T(8,128)(2,1)S(1)}, u32[]{:S(2)}, u32[]{:S(2)}) collective-permute-start(bf16[16,4096]{1,0:T(8,128)(2,1)S(1)} %fusion), channel_id=1, source_target_pairs={{0,44},{1,45},{2,46},{3,47},{4,48},{5,49},{6,50},{7,51},{8,52},{9,... | collective-permute-start | bytes 393224
  1383.7 43.5 %collective-permute-start.42 = (bf16[16,4096]{1,0:T(8,128)(2,1)S(1)}, bf16[16,4096]{1,0:T(8,128)(2,1)S(1)}, u32[]{:S(2)}, u32[]{:S(2)}) collective-permute-start(bf16[16,4096]{1,0:T(8,128)(2,1)S(1)} %fusion), channel_id=1, source_target_pairs={{0,43},{1,44},{2,45},{3,46},{4,47},{5,48},{6,49},{7,50},{8,51},{9,... | collective-permute-start | bytes 393224
  1391.0 39.1 %collective-permute-start.41 = (bf16[16,4096]{1,0:T(8,128)(2,1)S(1)}, bf16[16,4096]{1,0:T(8,128)(2,1)S(1)}, u32[]{:S(2)}, u32[]{:S(2)}) collective-permute-start(bf16[16,4096]{1,0:T(8,128)(2,1)S(1)} %fusion), channel_id=1, source_target_pairs={{0,42},{1,43},{2,44},{3,45},{4,46},{5,47},{6,48},{7,49},{8,50},{9,... | collective-permute-start | bytes 393224
  1408.9 30.7 %collective-permute-start.40 = (bf16[16,4096]{1,0:T(8,128)(2,1)S(1)}, bf16[16,4096]{1,0:T(8,128)(2,1)S(1)}, u32[]{:S(2)}, u32[]{:S(2)}) collective-permute-start(bf16[16,4096]{1,0:T(8,128)(2,1)S(1)} %fusion), channel_id=1, source_target_pairs={{0,41},{1,42},{2,43},{3,44},{4,45},{5,46},{6,47},{7,48},{8,49},{9,... | collective-permute-start | bytes 393224
  1414.7 27.6 %collective-permute-start.39 = (bf16[16,4096]{1,0:T(8,128)(2,1)S(1)}, bf16[16,4096]{1,0:T(8,128)(2,1)S(1)}, u32[]{:S(2)}, u32[]{:S(2)}) collective-permute-start(bf16[16,4096]{1,0:T(8,128)(2,1)S(1)} %fusion), channel_id=1, source_target_pairs={{0,40},{1,41},{2,42},{3,43},{4,44},{5,45},{6,46},{7,47},{8,48},{9,... | collective-permute-start | bytes 393224
  1416.6 27.6 %collective-permute-start.38 = (bf16[16,4096]{1,0:T(8,128)(2,1)S(1)}, bf16[16,4096]{1,0:T(8,128)(2,1)S(1)}, u32[]{:S(2)}, u32[]{:S(2)}) collective-permute-start(bf16[16,4096]{1,0:T(8,128)(2,1)S(1)} %fusion), channel_id=1, source_target_pairs={{0,39},{1,40},{2,41},{3,42},{4,43},{5,44},{6,45},{7,46},{8,47},{9,... | collective-permute-start | bytes 393224
  1427.2 26.1 %collective-permute-start.37 = (bf16[16,4096]{1,0:T(8,128)(2,1)S(1)}, bf16[16,4096]{1,0:T(8,128)(2,1)S(1)}, u32[]{:S(2)}, u32[]{:S(2)}) collective-permute-start(bf16[16,4096]{1,0:T(8,128)(2,1)S(1)} %fusion), channel_id=1, source_target_pairs={{0,38},{1,39},{2,40},{3,41},{4,42},{5,43},{6,44},{7,45},{8,46},{9,... | collective-permute-start | bytes 393224
  1430.1 26.5 %collective-permute-start.36 = (bf16[16,4096]{1,0:T(8,128)(2,1)S(1)}, bf16[16,4096]{1,0:T(8,128)(2,1)S(1)}, u32[]{:S(2)}, u32[]{:S(2)}) collective-permute-start(bf16[16,4096]{1,0:T(8,128)(2,1)S(1)} %fusion), channel_id=1, source_target_pairs={{0,37},{1,38},{2,39},{3,40},{4,41},{5,42},{6,43},{7,44},{8,45},{9,... | collective-permute-start | bytes 393224
  1439.6 19.0 collective-permute-start.35
  1442.3 18.2 collective-permute-start.34
  1444.2 23.9 %collective-permute-start.33 = (bf16[16,4096]{1,0:T(8,128)(2,1)S(1)}, bf16[16,4096]{1,0:T(8,128)(2,1)S(1)}, u32[]{:S(2)}, u32[]{:S(2)}) collective-permute-start(bf16[16,4096]{1,0:T(8,128)(2,1)S(1)} %fusion), channel_id=1, source_target_pairs={{0,34},{1,35},{2,36},{3,37},{4,38},{5,39},{6,40},{7,41},{8,42},{9,... | collective-permute-start | bytes 393224
  1453.2 37.0 %collective-permute-start.32 = (bf16[16,4096]{1,0:T(8,128)(2,1)S(1)}, bf16[16,4096]{1,0:T(8,128)(2,1)S(1)}, u32[]{:S(2)}, u32[]{:S(2)}) collective-permute-start(bf16[16,4096]{1,0:T(8,128)(2,1)S(1)} %fusion), channel_id=1, source_target_pairs={{0,33},{1,34},{2,35},{3,36},{4,37},{5,38},{6,39},{7,40},{8,41},{9,... | collective-permute-start | bytes 393224
  1456.6 46.7 %collective-permute-start.31 = (bf16[16,4096]{1,0:T(8,128)(2,1)S(1)}, bf16[16,4096]{1,0:T(8,128)(2,1)S(1)}, u32[]{:S(2)}, u32[]{:S(2)}) collective-permute-start(bf16[16,4096]{1,0:T(8,128)(2,1)S(1)} %fusion), channel_id=1, source_target_pairs={{0,32},{1,33},{2,34},{3,35},{4,36},{5,37},{6,38},{7,39},{8,40},{9,... | collective-permute-start | bytes 393224
  1458.6 57.9 %collective-permute-start.30 = (bf16[16,4096]{1,0:T(8,128)(2,1)S(1)}, bf16[16,4096]{1,0:T(8,128)(2,1)S(1)}, u32[]{:S(2)}, u32[]{:S(2)}) collective-permute-start(bf16[16,4096]{1,0:T(8,128)(2,1)S(1)} %fusion), channel_id=1, source_target_pairs={{0,31},{1,32},{2,33},{3,34},{4,35},{5,36},{6,37},{7,38},{8,39},{9,... | collective-permute-start | bytes 393224
  1460.5 69.1 %collective-permute-start.29 = (bf16[16,4096]{1,0:T(8,128)(2,1)S(1)}, bf16[16,4096]{1,0:T(8,128)(2,1)S(1)}, u32[]{:S(2)}, u32[]{:S(2)}) collective-permute-start(bf16[16,4096]{1,0:T(8,128)(2,1)S(1)} %fusion), channel_id=1, source_target_pairs={{0,30},{1,31},{2,32},{3,33},{4,34},{5,35},{6,36},{7,37},{8,38},{9,... | collective-permute-start | bytes 393224
  1468.1 74.7 %collective-permute-start.28 = (bf16[16,4096]{1,0:T(8,128)(2,1)S(1)}, bf16[16,4096]{1,0:T(8,128)(2,1)S(1)}, u32[]{:S(2)}, u32[]{:S(2)}) collective-permute-start(bf16[16,4096]{1,0:T(8,128)(2,1)S(1)} %fusion), channel_id=1, source_target_pairs={{0,29},{1,30},{2,31},{3,32},{4,33},{5,34},{6,35},{7,36},{8,37},{9,... | collective-permute-start | bytes 393224
  1490.2 65.7 %collective-permute-start.27 = (bf16[16,4096]{1,0:T(8,128)(2,1)S(1)}, bf16[16,4096]{1,0:T(8,128)(2,1)S(1)}, u32[]{:S(2)}, u32[]{:S(2)}) collective-permute-start(bf16[16,4096]{1,0:T(8,128)(2,1)S(1)} %fusion), channel_id=1, source_target_pairs={{0,28},{1,29},{2,30},{3,31},{4,32},{5,33},{6,34},{7,35},{8,36},{9,... | collective-permute-start | bytes 393224
  1503.4 65.7 %collective-permute-start.26 = (bf16[16,4096]{1,0:T(8,128)(2,1)S(1)}, bf16[16,4096]{1,0:T(8,128)(2,1)S(1)}, u32[]{:S(2)}, u32[]{:S(2)}) collective-permute-start(bf16[16,4096]{1,0:T(8,128)(2,1)S(1)} %fusion), channel_id=1, source_target_pairs={{0,27},{1,28},{2,29},{3,30},{4,31},{5,32},{6,33},{7,34},{8,35},{9,... | collective-permute-start | bytes 393224
  1516.5 65.7 %collective-permute-start.25 = (bf16[16,4096]{1,0:T(8,128)(2,1)S(1)}, bf16[16,4096]{1,0:T(8,128)(2,1)S(1)}, u32[]{:S(2)}, u32[]{:S(2)}) collective-permute-start(bf16[16,4096]{1,0:T(8,128)(2,1)S(1)} %fusion), channel_id=1, source_target_pairs={{0,26},{1,27},{2,28},{3,29},{4,30},{5,31},{6,32},{7,33},{8,34},{9,... | collective-permute-start | bytes 393224
  1529.7 65.7 %collective-permute-start.24 = (bf16[16,4096]{1,0:T(8,128)(2,1)S(1)}, bf16[16,4096]{1,0:T(8,128)(2,1)S(1)}, u32[]{:S(2)}, u32[]{:S(2)}) collective-permute-start(bf16[16,4096]{1,0:T(8,128)(2,1)S(1)} %fusion), channel_id=1, source_target_pairs={{0,25},{1,26},{2,27},{3,28},{4,29},{5,30},{6,31},{7,32},{8,33},{9,... | collective-permute-start | bytes 393224
  1542.8 65.7 %collective-permute-start.23 = (bf16[16,4096]{1,0:T(8,128)(2,1)S(1)}, bf16[16,4096]{1,0:T(8,128)(2,1)S(1)}, u32[]{:S(2)}, u32[]{:S(2)}) collective-permute-start(bf16[16,4096]{1,0:T(8,128)(2,1)S(1)} %fusion), channel_id=1, source_target_pairs={{0,24},{1,25},{2,26},{3,27},{4,28},{5,29},{6,30},{7,31},{8,32},{9,... | collective-permute-start | bytes 393224
  1556.0 65.7 %collective-permute-start.22 = (bf16[16,4096]{1,0:T(8,128)(2,1)S(1)}, bf16[16,4096]{1,0:T(8,128)(2,1)}, u32[]{:S(2)}, u32[]{:S(2)}) collective-permute-start(bf16[16,4096]{1,0:T(8,128)(2,1)S(1)} %fusion), channel_id=1, source_target_pairs={{0,23},{1,24},{2,25},{3,26},{4,27},{5,28},{6,29},{7,30},{8,31},{9,... | collective-permute-start | bytes 393224
  1569.1 65.7 %collective-permute-start.21 = (bf16[16,4096]{1,0:T(8,128)(2,1)S(1)}, bf16[16,4096]{1,0:T(8,128)(2,1)}, u32[]{:S(2)}, u32[]{:S(2)}) collective-permute-start(bf16[16,4096]{1,0:T(8,128)(2,1)S(1)} %fusion), channel_id=1, source_target_pairs={{0,22},{1,23},{2,24},{3,25},{4,26},{5,27},{6,28},{7,29},{8,30},{9,... | collective-permute-start | bytes 393224
  1582.3 65.7 %collective-permute-start.20 = (bf16[16,4096]{1,0:T(8,128)(2,1)S(1)}, bf16[16,4096]{1,0:T(8,128)(2,1)}, u32[]{:S(2)}, u32[]{:S(2)}) collective-permute-start(bf16[16,4096]{1,0:T(8,128)(2,1)S(1)} %fusion), channel_id=1, source_target_pairs={{0,21},{1,22},{2,23},{3,24},{4,25},{5,26},{6,27},{7,28},{8,29},{9,... | collective-permute-start | bytes 393224
  1595.4 65.7 %collective-permute-start.19 = (bf16[16,4096]{1,0:T(8,128)(2,1)S(1)}, bf16[16,4096]{1,0:T(8,128)(2,1)}, u32[]{:S(2)}, u32[]{:S(2)}) collective-permute-start(bf16[16,4096]{1,0:T(8,128)(2,1)S(1)} %fusion), channel_id=1, source_target_pairs={{0,20},{1,21},{2,22},{3,23},{4,24},{5,25},{6,26},{7,27},{8,28},{9,... | collective-permute-start | bytes 393224
  1608.6 65.7 %collective-permute-start.18 = (bf16[16,4096]{1,0:T(8,128)(2,1)S(1)}, bf16[16,4096]{1,0:T(8,128)(2,1)}, u32[]{:S(2)}, u32[]{:S(2)}) collective-permute-start(bf16[16,4096]{1,0:T(8,128)(2,1)S(1)} %fusion), channel_id=1, source_target_pairs={{0,19},{1,20},{2,21},{3,22},{4,23},{5,24},{6,25},{7,26},{8,27},{9,... | collective-permute-start | bytes 393224
  1621.7 65.7 %collective-permute-start.17 = (bf16[16,4096]{1,0:T(8,128)(2,1)S(1)}, bf16[16,4096]{1,0:T(8,128)(2,1)}, u32[]{:S(2)}, u32[]{:S(2)}) collective-permute-start(bf16[16,4096]{1,0:T(8,128)(2,1)S(1)} %fusion), channel_id=1, source_target_pairs={{0,18},{1,19},{2,20},{3,21},{4,22},{5,23},{6,24},{7,25},{8,26},{9,... | collective-permute-start | bytes 393224
  1634.9 65.7 %collective-permute-start.16 = (bf16[16,4096]{1,0:T(8,128)(2,1)S(1)}, bf16[16,4096]{1,0:T(8,128)(2,1)}, u32[]{:S(2)}, u32[]{:S(2)}) collective-permute-start(bf16[16,4096]{1,0:T(8,128)(2,1)S(1)} %fusion), channel_id=1, source_target_pairs={{0,17},{1,18},{2,19},{3,20},{4,21},{5,22},{6,23},{7,24},{8,25},{9,... | collective-permute-start | bytes 393224
  1648.0 65.7 %collective-permute-start.15 = (bf16[16,4096]{1,0:T(8,128)(2,1)S(1)}, bf16[16,4096]{1,0:T(8,128)(2,1)}, u32[]{:S(2)}, u32[]{:S(2)}) collective-permute-start(bf16[16,4096]{1,0:T(8,128)(2,1)S(1)} %fusion), channel_id=1, source_target_pairs={{0,16},{1,17},{2,18},{3,19},{4,20},{5,21},{6,22},{7,23},{8,24},{9,... | collective-permute-start | bytes 393224
  1661.2 67.4 %collective-permute-start.14 = (bf16[16,4096]{1,0:T(8,128)(2,1)S(1)}, bf16[16,4096]{1,0:T(8,128)(2,1)}, u32[]{:S(2)}, u32[]{:S(2)}) collective-permute-start(bf16[16,4096]{1,0:T(8,128)(2,1)S(1)} %fusion), channel_id=1, source_target_pairs={{0,15},{1,16},{2,17},{3,18},{4,19},{5,20},{6,21},{7,22},{8,23},{9,... | collective-permute-start | bytes 393224
  1674.3 67.4 %collective-permute-start.13 = (bf16[16,4096]{1,0:T(8,128)(2,1)S(1)}, bf16[16,4096]{1,0:T(8,128)(2,1)}, u32[]{:S(2)}, u32[]{:S(2)}) collective-permute-start(bf16[16,4096]{1,0:T(8,128)(2,1)S(1)} %fusion), channel_id=1, source_target_pairs={{0,14},{1,15},{2,16},{3,17},{4,18},{5,19},{6,20},{7,21},{8,22},{9,... | collective-permute-start | bytes 393224
  1687.4 67.4 %collective-permute-start.12 = (bf16[16,4096]{1,0:T(8,128)(2,1)S(1)}, bf16[16,4096]{1,0:T(8,128)(2,1)}, u32[]{:S(2)}, u32[]{:S(2)}) collective-permute-start(bf16[16,4096]{1,0:T(8,128)(2,1)S(1)} %fusion), channel_id=1, source_target_pairs={{0,13},{1,14},{2,15},{3,16},{4,17},{5,18},{6,19},{7,20},{8,21},{9,... | collective-permute-start | bytes 393224
  1700.6 67.4 %collective-permute-start.11 = (bf16[16,4096]{1,0:T(8,128)(2,1)S(1)}, bf16[16,4096]{1,0:T(8,128)(2,1)}, u32[]{:S(2)}, u32[]{:S(2)}) collective-permute-start(bf16[16,4096]{1,0:T(8,128)(2,1)S(1)} %fusion), channel_id=1, source_target_pairs={{0,12},{1,13},{2,14},{3,15},{4,16},{5,17},{6,18},{7,19},{8,20},{9,... | collective-permute-start | bytes 393224
  1714.1 67.0 %collective-permute-start.10 = (bf16[16,4096]{1,0:T(8,128)(2,1)S(1)}, bf16[16,4096]{1,0:T(8,128)(2,1)}, u32[]{:S(2)}, u32[]{:S(2)}) collective-permute-start(bf16[16,4096]{1,0:T(8,128)(2,1)S(1)} %fusion), channel_id=1, source_target_pairs={{0,11},{1,12},{2,13},{3,14},{4,15},{5,16},{6,17},{7,18},{8,19},{9,... | collective-permute-start | bytes 393224
  1728.6 68.6 %collective-permute-start.9 = (bf16[16,4096]{1,0:T(8,128)(2,1)S(1)}, bf16[16,4096]{1,0:T(8,128)(2,1)}, u32[]{:S(2)}, u32[]{:S(2)}) collective-permute-start(bf16[16,4096]{1,0:T(8,128)(2,1)S(1)} %fusion), channel_id=1, source_target_pairs={{0,10},{1,11},{2,12},{3,13},{4,14},{5,15},{6,16},{7,17},{8,18},{9,... | collective-permute-start | bytes 393224
  1741.7 68.6 %collective-permute-start.8 = (bf16[16,4096]{1,0:T(8,128)(2,1)S(1)}, bf16[16,4096]{1,0:T(8,128)(2,1)}, u32[]{:S(2)}, u32[]{:S(2)}) collective-permute-start(bf16[16,4096]{1,0:T(8,128)(2,1)S(1)} %fusion), channel_id=1, source_target_pairs={{0,9},{1,10},{2,11},{3,12},{4,13},{5,14},{6,15},{7,16},{8,17},{9,1... | collective-permute-start | bytes 393224
  1754.9 68.6 %collective-permute-start.7 = (bf16[16,4096]{1,0:T(8,128)(2,1)S(1)}, bf16[16,4096]{1,0:T(8,128)(2,1)}, u32[]{:S(2)}, u32[]{:S(2)}) collective-permute-start(bf16[16,4096]{1,0:T(8,128)(2,1)S(1)} %fusion), channel_id=1, source_target_pairs={{0,8},{1,9},{2,10},{3,11},{4,12},{5,13},{6,14},{7,15},{8,16},{9,17... | collective-permute-start | bytes 393224
  1768.0 68.6 %collective-permute-start.6 = (bf16[16,4096]{1,0:T(8,128)(2,1)S(1)}, bf16[16,4096]{1,0:T(8,128)(2,1)}, u32[]{:S(2)}, u32[]{:S(2)}) collective-permute-start(bf16[16,4096]{1,0:T(8,128)(2,1)S(1)} %fusion), channel_id=1, source_target_pairs={{0,7},{1,8},{2,9},{3,10},{4,11},{5,12},{6,13},{7,14},{8,15},{9,16}... | collective-permute-start | bytes 393224
  1781.1 68.6 %collective-permute-start.5 = (bf16[16,4096]{1,0:T(8,128)(2,1)S(1)}, bf16[16,4096]{1,0:T(8,128)(2,1)}, u32[]{:S(2)}, u32[]{:S(2)}) collective-permute-start(bf16[16,4096]{1,0:T(8,128)(2,1)S(1)} %fusion), channel_id=1, source_target_pairs={{0,6},{1,7},{2,8},{3,9},{4,10},{5,11},{6,12},{7,13},{8,14},{9,15},... | collective-permute-start | bytes 393224
  1797.2 66.2 %collective-permute-start.4 = (bf16[16,4096]{1,0:T(8,128)(2,1)S(1)}, bf16[16,4096]{1,0:T(8,128)(2,1)S(1)}, u32[]{:S(2)}, u32[]{:S(2)}) collective-permute-start(bf16[16,4096]{1,0:T(8,128)(2,1)S(1)} %fusion), channel_id=1, source_target_pairs={{0,5},{1,6},{2,7},{3,8},{4,9},{5,10},{6,11},{7,12},{8,13},{9,14},{... | collective-permute-start | bytes 393224
  1810.3 53.1 %collective-permute-start.3 = (bf16[16,4096]{1,0:T(8,128)(2,1)S(1)}, bf16[16,4096]{1,0:T(8,128)(2,1)S(1)}, u32[]{:S(2)}, u32[]{:S(2)}) collective-permute-start(bf16[16,4096]{1,0:T(8,128)(2,1)S(1)} %fusion), channel_id=1, source_target_pairs={{0,4},{1,5},{2,6},{3,7},{4,8},{5,9},{6,10},{7,11},{8,12},{9,13},{1... | collective-permute-start | bytes 393224
  1823.5 39.9 %collective-permute-start.2 = (bf16[16,4096]{1,0:T(8,128)(2,1)S(1)}, bf16[16,4096]{1,0:T(8,128)(2,1)S(1)}, u32[]{:S(2)}, u32[]{:S(2)}) collective-permute-start(bf16[16,4096]{1,0:T(8,128)(2,1)S(1)} %fusion), channel_id=1, source_target_pairs={{0,3},{1,4},{2,5},{3,6},{4,7},{5,8},{6,9},{7,10},{8,11},{9,12},{10... | collective-permute-start | bytes 393224
  1836.6 26.8 %collective-permute-start.1 = (bf16[16,4096]{1,0:T(8,128)(2,1)S(1)}, bf16[16,4096]{1,0:T(8,128)(2,1)S(1)}, u32[]{:S(2)}, u32[]{:S(2)}) collective-permute-start(bf16[16,4096]{1,0:T(8,128)(2,1)S(1)} %fusion), channel_id=1, source_target_pairs={{0,2},{1,3},{2,4},{3,5},{4,6},{5,7},{6,8},{7,9},{8,10},{9,11},{10,... | collective-permute-start | bytes 393224
  1849.8 22.7 %collective-permute-start = (bf16[16,4096]{1,0:T(8,128)(2,1)S(1)}, bf16[16,4096]{1,0:T(8,128)(2,1)}, u32[]{:S(2)}, u32[]{:S(2)}) collective-permute-start(bf16[16,4096]{1,0:T(8,128)(2,1)S(1)} %fusion), channel_id=1, source_target_pairs={{0,1},{1,2},{2,3},{3,4},{4,5},{5,6},{6,7},{7,8},{8,9},{9,10},{10,1... | collective-permute-start | bytes 393224
  (45 other events, 11512.2 us)
Sparse Core Ops, SparseCore 0:
  9.9 447.0 all-gather.3
where the time goes:
time: 2050 us; the launch traced here: 2040 us
  blocking collectives  998 us (49%)
  starting transfers between devices  531 us (26%)
  waiting for transfers between devices  232 us (11%)
  local copies, waits for them, and re-layouts  211 us (10%)
  matrix products  49.2 us (2%)
    unnamed x1, blocking collectives  661 us
    unnamed x64, starting transfers between devices  531 us
    all_gather x1, blocking collectives, on_device(): all_dense = lax.all_gather(dense, BOTH, axis=0, tiled=True)  337 us
    unnamed x95, local copies, waits for them, and re-layouts  206 us
    unnamed x65, waiting for transfers between devices  128 us
    all_gather x1, waiting for transfers between devices, on_device(): all_tokens = lax.all_gather(tokens, BOTH, axis=0, tiled=True)  104 us
  transfers between devices with their start and end apart: 65, of which 22 were waited for; matrix products, arithmetic and copies ran while one was open for 1% of the time, Pallas kernels for 0%

commit v1 on v0

--- a/solution.py
+++ b/solution.py
@@ -23,7 +23,8 @@
     experts = jnp.arange(experts_all, dtype=jnp.int32)
     dense = jnp.sum(jnp.where(expert_ids[..., None] == experts, gate_probs[..., None], 0.0), 1)
     all_tokens = lax.all_gather(tokens, BOTH, axis=0, tiled=True)
-    all_dense = lax.all_gather(dense, BOTH, axis=0, tiled=True)
+    outgoing = jnp.stack([dense] * lax.axis_size(BOTH))
+    all_dense = jnp.concatenate(lax.all_to_all(outgoing, BOTH, 0, 0), axis=0)
     load = planned_load(jnp.sum(all_dense, 0), swap_slot, per_device, owners, all_tokens.shape[0])
     mine = lax.dynamic_slice_in_dim(all_dense, lax.axis_index("expert") * per_device, per_device, 1)
     parts = []

time: 2050 us -> 2060 us (level)
  blocking collectives: 998 us -> 662 us
  waiting for transfers between devices: 232 us -> 553 us
    all_gather x1 -> x0, blocking collectives: 337 us -> none  [on_device(): all_dense = lax.all_gather(dense, BOTH, axis=0, tiled=True)]
    all_gather x1, waiting for transfers between devices: 104 us -> 395 us  [on_device(): all_tokens = lax.all_gather(tokens, BOTH, axis=0, tiled=True)]
    all_to_all x0 -> x1, waiting for transfers between devices: none -> 28.2 us  [on_device(): all_dense = jnp.concatenate(lax.all_to_all(outgoing, BOTH, 0, 0), axis=0)]
    unnamed x95 -> x96, local copies, waits for them, and re-layouts: 206 us -> 210 us
  transfers between devices with their start and end apart: 65 -> 66, of which waited for: 22 -> 23; matrix products, arithmetic and copies ran while one was open for 1% -> 1% of each run, Pallas kernels for 0% -> 0%
where the time goes in v1:
time: 2060 us; the launch traced here: 2050 us
  blocking collectives  662 us (32%)
  waiting for transfers between devices  553 us (27%)
  starting transfers between devices  536 us (26%)
  local copies, waits for them, and re-layouts  219 us (11%)
  matrix products  49.3 us (2%)
    unnamed x1, blocking collectives  662 us
    unnamed x64, starting transfers between devices  521 us
    all_gather x1, waiting for transfers between devices, on_device(): all_tokens = lax.all_gather(tokens, BOTH, axis=0, tiled=True)  395 us
    unnamed x96, local copies, waits for them, and re-layouts  210 us
    unnamed x65, waiting for transfers between devices  129 us
  transfers between devices with their start and end apart: 66, of which 23 were waited for; matrix products, arithmetic and copies ran while one was open for 1% of the time, Pallas kernels for 0%

profile of v1, /device:TPU:6, one launch (start us, length us, event | category | flops | bytes accessed | tf_op | source)
XLA Modules:
  0.0 2047.1 jit_solution(14832558013695053929)
XLA Ops:
  11.2 3.2 reshape.63
  14.4 15.5 all-to-all-start
  29.9 28.2 %all-to-all-done = f32[256,1,768]{2,1,0:T(1,128)} async-done(((f32[256,1,768]{2,1,0:T(1,128)}), f32[256,1,768]{2,1,0:T(1,128)}, u32[]{:S(2)}, u32[]{:S(2)}) %all-to-all-start) | async-done | bytes 786464 | tf_op jit(solution)/shard_map/all_to_all | solution.py:27
  58.6 4.5 reduce.5
  63.1 2.7 reshape.64
  65.9 2.5 reshape.56
  68.4 3.6 dynamic-slice_reduce_fusion.1
  72.0 395.4 %all-gather.3.cloned.1.call-done = bf16[256,12,4096]{2,1,0:T(8,128)(2,1)} async-done(((bf16[1,12,4096]{2,1,0:T(8,128)(2,1)}), bf16[256,12,4096]{2,1,0:T(8,128)(2,1)}) %all-gather.3.cloned.1.call-update) | async-done | bytes 25165840 | tf_op jit(solution)/shard_map/all_gather | solution.py:25
  467.4 34.8 %reshape.60 = bf16[3072,4096]{1,0:T(8,128)(2,1)} reshape(bf16[256,12,4096]{2,1,0:T(8,128)(2,1)} %all-gather.3.cloned.1.call-done) | data formatting | bytes 50331648
  502.2 14.5 fusion.1
  516.8 16.4 fusion.3
  533.1 4.3 fusion.8
  537.4 18.5 convolution_convert_fusion
  555.9 661.7 %fusion = bf16[16,4096]{1,0:T(8,128)(2,1)S(1)} fusion(bf16[3072,4096]{1,0:T(8,128)(2,1)} %convolution_convert_fusion), kind=kCustom, calls=%all-reduce-scatter | all-reduce-scatter fusion | flops 16777216 | bytes 25296896
  1217.6 77.1 %collective-permute-start.62 = (bf16[16,4096]{1,0:T(8,128)(2,1)S(1)}, bf16[16,4096]{1,0:T(8,128)(2,1)S(1)}, u32[]{:S(2)}, u32[]{:S(2)}) collective-permute-start(bf16[16,4096]{1,0:T(8,128)(2,1)S(1)} %fusion), channel_id=1, source_target_pairs={{0,63},{1,64},{2,65},{3,66},{4,67},{5,68},{6,69},{7,70},{8,71},{9,... | collective-permute-start | bytes 393224
  1299.9 1.9 collective-permute-start.59
  1301.8 7.3 collective-permute-done.63
  1311.0 1.9 collective-permute-start.57
  1314.9 1.9 collective-permute-start.55
  1322.1 25.9 %collective-permute-done.57 = bf16[16,4096]{1,0:T(8,128)(2,1)S(1)} collective-permute-done((bf16[16,4096]{1,0:T(8,128)(2,1)S(1)}, bf16[16,4096]{1,0:T(8,128)(2,1)S(1)}, u32[]{:S(2)}, u32[]{:S(2)}) %collective-permute-start.57) | collective-permute-done | bytes 131104
  1349.9 16.6 collective-permute-done.56
  1376.9 4.6 collective-permute-done.52
  1383.4 2.3 collective-permute-done.51
  1389.6 1.9 collective-permute-start.44
  1396.6 5.4 collective-permute-done.46
  1403.9 16.0 collective-permute-done.45
  1421.8 3.9 collective-permute-done.44
  1427.6 1.9 collective-permute-start.38
  1429.6 8.6 collective-permute-done.42
  1443.0 7.6 collective-permute-done.40
  1457.1 7.1 collective-permute-done.37
  1471.5 1.9 collective-permute-start.29
  1473.5 7.0 collective-permute-done.33
  1482.4 23.0 %collective-permute-start.27 = (bf16[16,4096]{1,0:T(8,128)(2,1)S(1)}, bf16[16,4096]{1,0:T(8,128)(2,1)S(1)}, u32[]{:S(2)}, u32[]{:S(2)}) collective-permute-start(bf16[16,4096]{1,0:T(8,128)(2,1)S(1)} %fusion), channel_id=1, source_target_pairs={{0,28},{1,29},{2,30},{3,31},{4,32},{5,33},{6,34},{7,35},{8,36},{9,... | collective-permute-start | bytes 393224
  1505.4 13.1 collective-permute-start.26
  1518.6 13.1 collective-permute-start.25
  1531.7 13.1 collective-permute-start.24
  1544.9 13.1 collective-permute-start.23
  1558.0 13.1 collective-permute-start.22
  1571.2 13.1 collective-permute-start.21
  1584.3 13.1 collective-permute-start.20
  1597.5 13.1 collective-permute-start.19
  1610.7 13.1 collective-permute-start.18
  1623.8 13.1 collective-permute-start.17
  1636.9 13.1 collective-permute-start.16
  1650.1 13.1 collective-permute-start.15
  1663.2 13.1 collective-permute-start.14
  1676.4 13.1 collective-permute-start.13
  1689.5 13.1 collective-permute-start.12
  1702.6 13.1 collective-permute-start.11
  1716.2 13.1 collective-permute-start.10
  1730.7 13.1 collective-permute-start.9
  1743.8 13.1 collective-permute-start.8
  1756.9 13.1 collective-permute-start.7
  1770.1 13.1 collective-permute-start.6
  1783.2 13.1 collective-permute-start.5
  1797.0 2.1 reduce_sum.28
  1799.3 13.1 collective-permute-start.4
  1812.4 13.1 collective-permute-start.3
  1825.5 13.1 collective-permute-start.2
  1838.7 13.1 collective-permute-start.1
  1851.8 13.1 collective-permute-start
  1866.9 7.6 collective-permute-done
  1874.5 164.2 %concatenate.4 = bf16[1036,4096]{1,0:T(8,128)(2,1)} concatenate(bf16[12,4096]{1,0:T(8,128)(2,1)} %copy-done.2, bf16[16,4096]{1,0:T(8,128)(2,1)S(1)} %collective-permute-done.62, bf16[16,4096]{1,0:T(8,128)(2,1)S(1)} %collective-permute-done.61, bf16[16,4096]{1,0:T(8,128)(2,1)} %copy-done.1, bf16[16,4096]{1,0:T(8,128)(2,1)} %copy-done.3, bf16[16,4096]{1,0:T(8,128)(2,1)} %copy-done.4, ...), dimensions={0} | concatenate | bytes 16973824
  (182 shorter events, 73.8 us)
Async XLA Ops:
  7.2 460.3 %all-gather.3.cloned.1.call-start = ((), (), s32[]{:S(2)}) async-start(), calls=%async_computation.1 | async-start | bytes 33685504 | tf_op jit(solution)/shard_map/all_gather | solution.py:25
  14.4 43.7 %all-to-all-start = ((f32[256,1,768]{2,1,0:T(1,128)}), f32[256,1,768]{2,1,0:T(1,128)}, u32[]{:S(2)}, u32[]{:S(2)}) async-start(f32[256,1,768]{2,1,0:T(1,128)} %reshape.63), calls=%async_computation | async-start | bytes 1572864 | tf_op jit(solution)/shard_map/all_to_all | solution.py:27
  1217.6 93.4 %collective-permute-start.62 = (bf16[16,4096]{1,0:T(8,128)(2,1)S(1)}, bf16[16,4096]{1,0:T(8,128)(2,1)S(1)}, u32[]{:S(2)}, u32[]{:S(2)}) collective-permute-start(bf16[16,4096]{1,0:T(8,128)(2,1)S(1)} %fusion), channel_id=1, source_target_pairs={{0,63},{1,64},{2,65},{3,66},{4,67},{5,68},{6,69},{7,70},{8,71},{9,... | collective-permute-start | bytes 393224
  1294.7 18.3 collective-permute-start.61
  1296.6 18.3 collective-permute-start.60
  1299.9 16.9 collective-permute-start.59
  1311.0 37.0 %collective-permute-start.57 = (bf16[16,4096]{1,0:T(8,128)(2,1)S(1)}, bf16[16,4096]{1,0:T(8,128)(2,1)S(1)}, u32[]{:S(2)}, u32[]{:S(2)}) collective-permute-start(bf16[16,4096]{1,0:T(8,128)(2,1)S(1)} %fusion), channel_id=1, source_target_pairs={{0,58},{1,59},{2,60},{3,61},{4,62},{5,63},{6,64},{7,65},{8,66},{9,... | collective-permute-start | bytes 393224
  1313.0 53.6 %collective-permute-start.56 = (bf16[16,4096]{1,0:T(8,128)(2,1)S(1)}, bf16[16,4096]{1,0:T(8,128)(2,1)S(1)}, u32[]{:S(2)}, u32[]{:S(2)}) collective-permute-start(bf16[16,4096]{1,0:T(8,128)(2,1)S(1)} %fusion), channel_id=1, source_target_pairs={{0,57},{1,58},{2,59},{3,60},{4,61},{5,62},{6,63},{7,64},{8,65},{9,... | collective-permute-start | bytes 393224
  1314.9 54.5 %collective-permute-start.55 = (bf16[16,4096]{1,0:T(8,128)(2,1)S(1)}, bf16[16,4096]{1,0:T(8,128)(2,1)S(1)}, u32[]{:S(2)}, u32[]{:S(2)}) collective-permute-start(bf16[16,4096]{1,0:T(8,128)(2,1)S(1)} %fusion), channel_id=1, source_target_pairs={{0,56},{1,57},{2,58},{3,59},{4,60},{5,61},{6,62},{7,63},{8,64},{9,... | collective-permute-start | bytes 393224
  1316.9 55.3 %collective-permute-start.54 = (bf16[16,4096]{1,0:T(8,128)(2,1)S(1)}, bf16[16,4096]{1,0:T(8,128)(2,1)S(1)}, u32[]{:S(2)}, u32[]{:S(2)}) collective-permute-start(bf16[16,4096]{1,0:T(8,128)(2,1)S(1)} %fusion), channel_id=1, source_target_pairs={{0,55},{1,56},{2,57},{3,58},{4,59},{5,60},{6,61},{7,62},{8,63},{9,... | collective-permute-start | bytes 393224
  1320.2 54.8 %collective-permute-start.53 = (bf16[16,4096]{1,0:T(8,128)(2,1)S(1)}, bf16[16,4096]{1,0:T(8,128)(2,1)S(1)}, u32[]{:S(2)}, u32[]{:S(2)}) collective-permute-start(bf16[16,4096]{1,0:T(8,128)(2,1)S(1)} %fusion), channel_id=1, source_target_pairs={{0,54},{1,55},{2,56},{3,57},{4,58},{5,59},{6,60},{7,61},{8,62},{9,... | collective-permute-start | bytes 393224
  1348.0 33.5 %collective-permute-start.52 = (bf16[16,4096]{1,0:T(8,128)(2,1)S(1)}, bf16[16,4096]{1,0:T(8,128)(2,1)S(1)}, u32[]{:S(2)}, u32[]{:S(2)}) collective-permute-start(bf16[16,4096]{1,0:T(8,128)(2,1)S(1)} %fusion), channel_id=1, source_target_pairs={{0,53},{1,54},{2,55},{3,56},{4,57},{5,58},{6,59},{7,60},{8,61},{9,... | collective-permute-start | bytes 393224
  1366.6 19.1 collective-permute-start.51
  1369.4 18.2 collective-permute-start.50
  1372.2 17.4 collective-permute-start.49
  1375.0 16.5 collective-permute-start.48
  1381.5 13.2 collective-permute-start.47
  1385.7 16.3 collective-permute-start.46
  1387.6 32.3 %collective-permute-start.45 = (bf16[16,4096]{1,0:T(8,128)(2,1)S(1)}, bf16[16,4096]{1,0:T(8,128)(2,1)S(1)}, u32[]{:S(2)}, u32[]{:S(2)}) collective-permute-start(bf16[16,4096]{1,0:T(8,128)(2,1)S(1)} %fusion), channel_id=1, source_target_pairs={{0,46},{1,47},{2,48},{3,49},{4,50},{5,51},{6,52},{7,53},{8,54},{9,... | collective-permute-start | bytes 393224
  1389.6 36.1 %collective-permute-start.44 = (bf16[16,4096]{1,0:T(8,128)(2,1)S(1)}, bf16[16,4096]{1,0:T(8,128)(2,1)S(1)}, u32[]{:S(2)}, u32[]{:S(2)}) collective-permute-start(bf16[16,4096]{1,0:T(8,128)(2,1)S(1)} %fusion), channel_id=1, source_target_pairs={{0,45},{1,46},{2,47},{3,48},{4,49},{5,50},{6,51},{7,52},{8,53},{9,... | collective-permute-start | bytes 393224
  1391.5 36.1 %collective-permute-start.43 = (bf16[16,4096]{1,0:T(8,128)(2,1)S(1)}, bf16[16,4096]{1,0:T(8,128)(2,1)S(1)}, u32[]{:S(2)}, u32[]{:S(2)}) collective-permute-start(bf16[16,4096]{1,0:T(8,128)(2,1)S(1)} %fusion), channel_id=1, source_target_pairs={{0,44},{1,45},{2,46},{3,47},{4,48},{5,49},{6,50},{7,51},{8,52},{9,... | collective-permute-start | bytes 393224
  1394.7 43.5 %collective-permute-start.42 = (bf16[16,4096]{1,0:T(8,128)(2,1)S(1)}, bf16[16,4096]{1,0:T(8,128)(2,1)S(1)}, u32[]{:S(2)}, u32[]{:S(2)}) collective-permute-start(bf16[16,4096]{1,0:T(8,128)(2,1)S(1)} %fusion), channel_id=1, source_target_pairs={{0,43},{1,44},{2,45},{3,46},{4,47},{5,48},{6,49},{7,50},{8,51},{9,... | collective-permute-start | bytes 393224
  1402.0 39.1 %collective-permute-start.41 = (bf16[16,4096]{1,0:T(8,128)(2,1)S(1)}, bf16[16,4096]{1,0:T(8,128)(2,1)S(1)}, u32[]{:S(2)}, u32[]{:S(2)}) collective-permute-start(bf16[16,4096]{1,0:T(8,128)(2,1)S(1)} %fusion), channel_id=1, source_target_pairs={{0,42},{1,43},{2,44},{3,45},{4,46},{5,47},{6,48},{7,49},{8,50},{9,... | collective-permute-start | bytes 393224
  1419.9 30.7 %collective-permute-start.40 = (bf16[16,4096]{1,0:T(8,128)(2,1)S(1)}, bf16[16,4096]{1,0:T(8,128)(2,1)S(1)}, u32[]{:S(2)}, u32[]{:S(2)}) collective-permute-start(bf16[16,4096]{1,0:T(8,128)(2,1)S(1)} %fusion), channel_id=1, source_target_pairs={{0,41},{1,42},{2,43},{3,44},{4,45},{5,46},{6,47},{7,48},{8,49},{9,... | collective-permute-start | bytes 393224
  1425.7 27.6 %collective-permute-start.39 = (bf16[16,4096]{1,0:T(8,128)(2,1)S(1)}, bf16[16,4096]{1,0:T(8,128)(2,1)S(1)}, u32[]{:S(2)}, u32[]{:S(2)}) collective-permute-start(bf16[16,4096]{1,0:T(8,128)(2,1)S(1)} %fusion), channel_id=1, source_target_pairs={{0,40},{1,41},{2,42},{3,43},{4,44},{5,45},{6,46},{7,47},{8,48},{9,... | collective-permute-start | bytes 393224
  1427.6 27.6 %collective-permute-start.38 = (bf16[16,4096]{1,0:T(8,128)(2,1)S(1)}, bf16[16,4096]{1,0:T(8,128)(2,1)S(1)}, u32[]{:S(2)}, u32[]{:S(2)}) collective-permute-start(bf16[16,4096]{1,0:T(8,128)(2,1)S(1)} %fusion), channel_id=1, source_target_pairs={{0,39},{1,40},{2,41},{3,42},{4,43},{5,44},{6,45},{7,46},{8,47},{9,... | collective-permute-start | bytes 393224
  1438.2 26.1 %collective-permute-start.37 = (bf16[16,4096]{1,0:T(8,128)(2,1)S(1)}, bf16[16,4096]{1,0:T(8,128)(2,1)S(1)}, u32[]{:S(2)}, u32[]{:S(2)}) collective-permute-start(bf16[16,4096]{1,0:T(8,128)(2,1)S(1)} %fusion), channel_id=1, source_target_pairs={{0,38},{1,39},{2,40},{3,41},{4,42},{5,43},{6,44},{7,45},{8,46},{9,... | collective-permute-start | bytes 393224
  1441.1 26.5 %collective-permute-start.36 = (bf16[16,4096]{1,0:T(8,128)(2,1)S(1)}, bf16[16,4096]{1,0:T(8,128)(2,1)S(1)}, u32[]{:S(2)}, u32[]{:S(2)}) collective-permute-start(bf16[16,4096]{1,0:T(8,128)(2,1)S(1)} %fusion), channel_id=1, source_target_pairs={{0,37},{1,38},{2,39},{3,40},{4,41},{5,42},{6,43},{7,44},{8,45},{9,... | collective-permute-start | bytes 393224
  1450.6 19.0 collective-permute-start.35
  1453.3 18.2 collective-permute-start.34
  1455.2 25.3 %collective-permute-start.33 = (bf16[16,4096]{1,0:T(8,128)(2,1)S(1)}, bf16[16,4096]{1,0:T(8,128)(2,1)S(1)}, u32[]{:S(2)}, u32[]{:S(2)}) collective-permute-start(bf16[16,4096]{1,0:T(8,128)(2,1)S(1)} %fusion), channel_id=1, source_target_pairs={{0,34},{1,35},{2,36},{3,37},{4,38},{5,39},{6,40},{7,41},{8,42},{9,... | collective-permute-start | bytes 393224
  1464.3 18.2 collective-permute-start.32
  1467.6 37.8 %collective-permute-start.31 = (bf16[16,4096]{1,0:T(8,128)(2,1)S(1)}, bf16[16,4096]{1,0:T(8,128)(2,1)S(1)}, u32[]{:S(2)}, u32[]{:S(2)}) collective-permute-start(bf16[16,4096]{1,0:T(8,128)(2,1)S(1)} %fusion), channel_id=1, source_target_pairs={{0,32},{1,33},{2,34},{3,35},{4,36},{5,37},{6,38},{7,39},{8,40},{9,... | collective-permute-start | bytes 393224
  1469.6 49.0 %collective-permute-start.30 = (bf16[16,4096]{1,0:T(8,128)(2,1)S(1)}, bf16[16,4096]{1,0:T(8,128)(2,1)S(1)}, u32[]{:S(2)}, u32[]{:S(2)}) collective-permute-start(bf16[16,4096]{1,0:T(8,128)(2,1)S(1)} %fusion), channel_id=1, source_target_pairs={{0,31},{1,32},{2,33},{3,34},{4,35},{5,36},{6,37},{7,38},{8,39},{9,... | collective-permute-start | bytes 393224
  1471.5 60.2 %collective-permute-start.29 = (bf16[16,4096]{1,0:T(8,128)(2,1)S(1)}, bf16[16,4096]{1,0:T(8,128)(2,1)S(1)}, u32[]{:S(2)}, u32[]{:S(2)}) collective-permute-start(bf16[16,4096]{1,0:T(8,128)(2,1)S(1)} %fusion), channel_id=1, source_target_pairs={{0,30},{1,31},{2,32},{3,33},{4,34},{5,35},{6,36},{7,37},{8,38},{9,... | collective-permute-start | bytes 393224
  1480.5 64.4 %collective-permute-start.28 = (bf16[16,4096]{1,0:T(8,128)(2,1)S(1)}, bf16[16,4096]{1,0:T(8,128)(2,1)S(1)}, u32[]{:S(2)}, u32[]{:S(2)}) collective-permute-start(bf16[16,4096]{1,0:T(8,128)(2,1)S(1)} %fusion), channel_id=1, source_target_pairs={{0,29},{1,30},{2,31},{3,32},{4,33},{5,34},{6,35},{7,36},{8,37},{9,... | collective-permute-start | bytes 393224
  1482.4 75.6 %collective-permute-start.27 = (bf16[16,4096]{1,0:T(8,128)(2,1)S(1)}, bf16[16,4096]{1,0:T(8,128)(2,1)S(1)}, u32[]{:S(2)}, u32[]{:S(2)}) collective-permute-start(bf16[16,4096]{1,0:T(8,128)(2,1)S(1)} %fusion), channel_id=1, source_target_pairs={{0,28},{1,29},{2,30},{3,31},{4,32},{5,33},{6,34},{7,35},{8,36},{9,... | collective-permute-start | bytes 393224
  1505.4 65.7 %collective-permute-start.26 = (bf16[16,4096]{1,0:T(8,128)(2,1)S(1)}, bf16[16,4096]{1,0:T(8,128)(2,1)S(1)}, u32[]{:S(2)}, u32[]{:S(2)}) collective-permute-start(bf16[16,4096]{1,0:T(8,128)(2,1)S(1)} %fusion), channel_id=1, source_target_pairs={{0,27},{1,28},{2,29},{3,30},{4,31},{5,32},{6,33},{7,34},{8,35},{9,... | collective-permute-start | bytes 393224
  1518.6 65.7 %collective-permute-start.25 = (bf16[16,4096]{1,0:T(8,128)(2,1)S(1)}, bf16[16,4096]{1,0:T(8,128)(2,1)S(1)}, u32[]{:S(2)}, u32[]{:S(2)}) collective-permute-start(bf16[16,4096]{1,0:T(8,128)(2,1)S(1)} %fusion), channel_id=1, source_target_pairs={{0,26},{1,27},{2,28},{3,29},{4,30},{5,31},{6,32},{7,33},{8,34},{9,... | collective-permute-start | bytes 393224
  1531.7 65.7 %collective-permute-start.24 = (bf16[16,4096]{1,0:T(8,128)(2,1)S(1)}, bf16[16,4096]{1,0:T(8,128)(2,1)S(1)}, u32[]{:S(2)}, u32[]{:S(2)}) collective-permute-start(bf16[16,4096]{1,0:T(8,128)(2,1)S(1)} %fusion), channel_id=1, source_target_pairs={{0,25},{1,26},{2,27},{3,28},{4,29},{5,30},{6,31},{7,32},{8,33},{9,... | collective-permute-start | bytes 393224
  1544.9 65.7 %collective-permute-start.23 = (bf16[16,4096]{1,0:T(8,128)(2,1)S(1)}, bf16[16,4096]{1,0:T(8,128)(2,1)S(1)}, u32[]{:S(2)}, u32[]{:S(2)}) collective-permute-start(bf16[16,4096]{1,0:T(8,128)(2,1)S(1)} %fusion), channel_id=1, source_target_pairs={{0,24},{1,25},{2,26},{3,27},{4,28},{5,29},{6,30},{7,31},{8,32},{9,... | collective-permute-start | bytes 393224
  1558.0 65.7 %collective-permute-start.22 = (bf16[16,4096]{1,0:T(8,128)(2,1)S(1)}, bf16[16,4096]{1,0:T(8,128)(2,1)}, u32[]{:S(2)}, u32[]{:S(2)}) collective-permute-start(bf16[16,4096]{1,0:T(8,128)(2,1)S(1)} %fusion), channel_id=1, source_target_pairs={{0,23},{1,24},{2,25},{3,26},{4,27},{5,28},{6,29},{7,30},{8,31},{9,... | collective-permute-start | bytes 393224
  1571.2 65.7 %collective-permute-start.21 = (bf16[16,4096]{1,0:T(8,128)(2,1)S(1)}, bf16[16,4096]{1,0:T(8,128)(2,1)}, u32[]{:S(2)}, u32[]{:S(2)}) collective-permute-start(bf16[16,4096]{1,0:T(8,128)(2,1)S(1)} %fusion), channel_id=1, source_target_pairs={{0,22},{1,23},{2,24},{3,25},{4,26},{5,27},{6,28},{7,29},{8,30},{9,... | collective-permute-start | bytes 393224
  1584.3 65.7 %collective-permute-start.20 = (bf16[16,4096]{1,0:T(8,128)(2,1)S(1)}, bf16[16,4096]{1,0:T(8,128)(2,1)}, u32[]{:S(2)}, u32[]{:S(2)}) collective-permute-start(bf16[16,4096]{1,0:T(8,128)(2,1)S(1)} %fusion), channel_id=1, source_target_pairs={{0,21},{1,22},{2,23},{3,24},{4,25},{5,26},{6,27},{7,28},{8,29},{9,... | collective-permute-start | bytes 393224
  1597.5 65.7 %collective-permute-start.19 = (bf16[16,4096]{1,0:T(8,128)(2,1)S(1)}, bf16[16,4096]{1,0:T(8,128)(2,1)}, u32[]{:S(2)}, u32[]{:S(2)}) collective-permute-start(bf16[16,4096]{1,0:T(8,128)(2,1)S(1)} %fusion), channel_id=1, source_target_pairs={{0,20},{1,21},{2,22},{3,23},{4,24},{5,25},{6,26},{7,27},{8,28},{9,... | collective-permute-start | bytes 393224
  1610.7 65.7 %collective-permute-start.18 = (bf16[16,4096]{1,0:T(8,128)(2,1)S(1)}, bf16[16,4096]{1,0:T(8,128)(2,1)}, u32[]{:S(2)}, u32[]{:S(2)}) collective-permute-start(bf16[16,4096]{1,0:T(8,128)(2,1)S(1)} %fusion), channel_id=1, source_target_pairs={{0,19},{1,20},{2,21},{3,22},{4,23},{5,24},{6,25},{7,26},{8,27},{9,... | collective-permute-start | bytes 393224
  1623.8 65.7 %collective-permute-start.17 = (bf16[16,4096]{1,0:T(8,128)(2,1)S(1)}, bf16[16,4096]{1,0:T(8,128)(2,1)}, u32[]{:S(2)}, u32[]{:S(2)}) collective-permute-start(bf16[16,4096]{1,0:T(8,128)(2,1)S(1)} %fusion), channel_id=1, source_target_pairs={{0,18},{1,19},{2,20},{3,21},{4,22},{5,23},{6,24},{7,25},{8,26},{9,... | collective-permute-start | bytes 393224
  1636.9 65.7 %collective-permute-start.16 = (bf16[16,4096]{1,0:T(8,128)(2,1)S(1)}, bf16[16,4096]{1,0:T(8,128)(2,1)}, u32[]{:S(2)}, u32[]{:S(2)}) collective-permute-start(bf16[16,4096]{1,0:T(8,128)(2,1)S(1)} %fusion), channel_id=1, source_target_pairs={{0,17},{1,18},{2,19},{3,20},{4,21},{5,22},{6,23},{7,24},{8,25},{9,... | collective-permute-start | bytes 393224
  1650.1 65.7 %collective-permute-start.15 = (bf16[16,4096]{1,0:T(8,128)(2,1)S(1)}, bf16[16,4096]{1,0:T(8,128)(2,1)}, u32[]{:S(2)}, u32[]{:S(2)}) collective-permute-start(bf16[16,4096]{1,0:T(8,128)(2,1)S(1)} %fusion), channel_id=1, source_target_pairs={{0,16},{1,17},{2,18},{3,19},{4,20},{5,21},{6,22},{7,23},{8,24},{9,... | collective-permute-start | bytes 393224
  1663.2 67.4 %collective-permute-start.14 = (bf16[16,4096]{1,0:T(8,128)(2,1)S(1)}, bf16[16,4096]{1,0:T(8,128)(2,1)}, u32[]{:S(2)}, u32[]{:S(2)}) collective-permute-start(bf16[16,4096]{1,0:T(8,128)(2,1)S(1)} %fusion), channel_id=1, source_target_pairs={{0,15},{1,16},{2,17},{3,18},{4,19},{5,20},{6,21},{7,22},{8,23},{9,... | collective-permute-start | bytes 393224
  1676.4 67.4 %collective-permute-start.13 = (bf16[16,4096]{1,0:T(8,128)(2,1)S(1)}, bf16[16,4096]{1,0:T(8,128)(2,1)}, u32[]{:S(2)}, u32[]{:S(2)}) collective-permute-start(bf16[16,4096]{1,0:T(8,128)(2,1)S(1)} %fusion), channel_id=1, source_target_pairs={{0,14},{1,15},{2,16},{3,17},{4,18},{5,19},{6,20},{7,21},{8,22},{9,... | collective-permute-start | bytes 393224
  1689.5 67.4 %collective-permute-start.12 = (bf16[16,4096]{1,0:T(8,128)(2,1)S(1)}, bf16[16,4096]{1,0:T(8,128)(2,1)}, u32[]{:S(2)}, u32[]{:S(2)}) collective-permute-start(bf16[16,4096]{1,0:T(8,128)(2,1)S(1)} %fusion), channel_id=1, source_target_pairs={{0,13},{1,14},{2,15},{3,16},{4,17},{5,18},{6,19},{7,20},{8,21},{9,... | collective-permute-start | bytes 393224
  1702.6 67.4 %collective-permute-start.11 = (bf16[16,4096]{1,0:T(8,128)(2,1)S(1)}, bf16[16,4096]{1,0:T(8,128)(2,1)}, u32[]{:S(2)}, u32[]{:S(2)}) collective-permute-start(bf16[16,4096]{1,0:T(8,128)(2,1)S(1)} %fusion), channel_id=1, source_target_pairs={{0,12},{1,13},{2,14},{3,15},{4,16},{5,17},{6,18},{7,19},{8,20},{9,... | collective-permute-start | bytes 393224
  1716.2 67.0 %collective-permute-start.10 = (bf16[16,4096]{1,0:T(8,128)(2,1)S(1)}, bf16[16,4096]{1,0:T(8,128)(2,1)}, u32[]{:S(2)}, u32[]{:S(2)}) collective-permute-start(bf16[16,4096]{1,0:T(8,128)(2,1)S(1)} %fusion), channel_id=1, source_target_pairs={{0,11},{1,12},{2,13},{3,14},{4,15},{5,16},{6,17},{7,18},{8,19},{9,... | collective-permute-start | bytes 393224
  1730.7 68.6 %collective-permute-start.9 = (bf16[16,4096]{1,0:T(8,128)(2,1)S(1)}, bf16[16,4096]{1,0:T(8,128)(2,1)}, u32[]{:S(2)}, u32[]{:S(2)}) collective-permute-start(bf16[16,4096]{1,0:T(8,128)(2,1)S(1)} %fusion), channel_id=1, source_target_pairs={{0,10},{1,11},{2,12},{3,13},{4,14},{5,15},{6,16},{7,17},{8,18},{9,... | collective-permute-start | bytes 393224
  1743.8 68.6 %collective-permute-start.8 = (bf16[16,4096]{1,0:T(8,128)(2,1)S(1)}, bf16[16,4096]{1,0:T(8,128)(2,1)}, u32[]{:S(2)}, u32[]{:S(2)}) collective-permute-start(bf16[16,4096]{1,0:T(8,128)(2,1)S(1)} %fusion), channel_id=1, source_target_pairs={{0,9},{1,10},{2,11},{3,12},{4,13},{5,14},{6,15},{7,16},{8,17},{9,1... | collective-permute-start | bytes 393224
  1756.9 68.6 %collective-permute-start.7 = (bf16[16,4096]{1,0:T(8,128)(2,1)S(1)}, bf16[16,4096]{1,0:T(8,128)(2,1)}, u32[]{:S(2)}, u32[]{:S(2)}) collective-permute-start(bf16[16,4096]{1,0:T(8,128)(2,1)S(1)} %fusion), channel_id=1, source_target_pairs={{0,8},{1,9},{2,10},{3,11},{4,12},{5,13},{6,14},{7,15},{8,16},{9,17... | collective-permute-start | bytes 393224
  1770.1 68.6 %collective-permute-start.6 = (bf16[16,4096]{1,0:T(8,128)(2,1)S(1)}, bf16[16,4096]{1,0:T(8,128)(2,1)}, u32[]{:S(2)}, u32[]{:S(2)}) collective-permute-start(bf16[16,4096]{1,0:T(8,128)(2,1)S(1)} %fusion), channel_id=1, source_target_pairs={{0,7},{1,8},{2,9},{3,10},{4,11},{5,12},{6,13},{7,14},{8,15},{9,16}... | collective-permute-start | bytes 393224
  1783.2 68.6 %collective-permute-start.5 = (bf16[16,4096]{1,0:T(8,128)(2,1)S(1)}, bf16[16,4096]{1,0:T(8,128)(2,1)}, u32[]{:S(2)}, u32[]{:S(2)}) collective-permute-start(bf16[16,4096]{1,0:T(8,128)(2,1)S(1)} %fusion), channel_id=1, source_target_pairs={{0,6},{1,7},{2,8},{3,9},{4,10},{5,11},{6,12},{7,13},{8,14},{9,15},... | collective-permute-start | bytes 393224
  1799.3 66.2 %collective-permute-start.4 = (bf16[16,4096]{1,0:T(8,128)(2,1)S(1)}, bf16[16,4096]{1,0:T(8,128)(2,1)S(1)}, u32[]{:S(2)}, u32[]{:S(2)}) collective-permute-start(bf16[16,4096]{1,0:T(8,128)(2,1)S(1)} %fusion), channel_id=1, source_target_pairs={{0,5},{1,6},{2,7},{3,8},{4,9},{5,10},{6,11},{7,12},{8,13},{9,14},{... | collective-permute-start | bytes 393224
  1812.4 53.1 %collective-permute-start.3 = (bf16[16,4096]{1,0:T(8,128)(2,1)S(1)}, bf16[16,4096]{1,0:T(8,128)(2,1)S(1)}, u32[]{:S(2)}, u32[]{:S(2)}) collective-permute-start(bf16[16,4096]{1,0:T(8,128)(2,1)S(1)} %fusion), channel_id=1, source_target_pairs={{0,4},{1,5},{2,6},{3,7},{4,8},{5,9},{6,10},{7,11},{8,12},{9,13},{1... | collective-permute-start | bytes 393224
  1825.5 39.9 %collective-permute-start.2 = (bf16[16,4096]{1,0:T(8,128)(2,1)S(1)}, bf16[16,4096]{1,0:T(8,128)(2,1)S(1)}, u32[]{:S(2)}, u32[]{:S(2)}) collective-permute-start(bf16[16,4096]{1,0:T(8,128)(2,1)S(1)} %fusion), channel_id=1, source_target_pairs={{0,3},{1,4},{2,5},{3,6},{4,7},{5,8},{6,9},{7,10},{8,11},{9,12},{10... | collective-permute-start | bytes 393224
  1838.7 26.8 %collective-permute-start.1 = (bf16[16,4096]{1,0:T(8,128)(2,1)S(1)}, bf16[16,4096]{1,0:T(8,128)(2,1)S(1)}, u32[]{:S(2)}, u32[]{:S(2)}) collective-permute-start(bf16[16,4096]{1,0:T(8,128)(2,1)S(1)} %fusion), channel_id=1, source_target_pairs={{0,2},{1,3},{2,4},{3,5},{4,6},{5,7},{6,8},{7,9},{8,10},{9,11},{10,... | collective-permute-start | bytes 393224
  1851.8 22.7 %collective-permute-start = (bf16[16,4096]{1,0:T(8,128)(2,1)S(1)}, bf16[16,4096]{1,0:T(8,128)(2,1)}, u32[]{:S(2)}, u32[]{:S(2)}) collective-permute-start(bf16[16,4096]{1,0:T(8,128)(2,1)S(1)} %fusion), channel_id=1, source_target_pairs={{0,1},{1,2},{2,3},{3,4},{4,5},{5,6},{6,7},{7,8},{8,9},{9,10},{10,1... | collective-permute-start | bytes 393224
  (46 other events, 11282.7 us)
Sparse Core Ops, SparseCore 0:
  9.9 457.4 all-gather.2
